TPU v7x, 32 devices: a whole 2x2x4 slice. The times are simulated.
32 devices in a mesh: ex: 8 (over z, x), tp: 4 (over y, core).
Axes of the slice: x: 2, y: 2, z: 4, core: 2. Of those that a mesh axis runs over, the one named last changes fastest.
Arguments:
- inputs: bfloat16 [1024, 768], P('ex'), may hold values from -6 to 6
- routes: int32 [1024, 2], P('ex'), may hold values from 0 to 7, all different within a row; in each aligned block of 128 rows (0 to 127, 128 to 255, ...) at most 64 rows name the same one
- lengths: int32 [8, 4], P('ex'), may hold values from 1 to 96, 128 in all within a row
- w_query: bfloat16 [768, 768], P(None, 'tp'), may hold values from -0.21875 to 0.21875
- w_key: bfloat16 [768, 768], P(None, 'tp'), may hold values from -0.21875 to 0.21875
- w_value: bfloat16 [768, 768], P(None, 'tp'), may hold values from -0.21875 to 0.21875
- w_attn_out: bfloat16 [768, 768], P('tp'), may hold values from -0.875 to 0.875
- gain_attn: float32 [768], replicated, may hold values from 0.25 to 1.75
- gain_moe: float32 [768], replicated, may hold values from 0.25 to 1.75
- rel_bias: float32 [32, 12], P(None, 'tp'), may hold values from -4 to 4
- w_router: bfloat16 [768, 8], replicated, may hold values from -0.15625 to 0.15625
- w_in: bfloat16 [8, 768, 3072], P('ex', None, 'tp'), may hold values from -0.21875 to 0.21875
- w_out: bfloat16 [8, 3072, 768], P('ex', 'tp'), may hold values from -0.109375 to 0.109375
- cotangent: bfloat16 [1024, 768], P('ex'), may hold values from -6 to 6
Outputs:
- output: bfloat16 [1024, 768], P('ex')
- grad_inputs: bfloat16 [1024, 768], P('ex')
- grad_w_query: float32 [768, 768], P(None, 'tp')
- grad_w_key: float32 [768, 768], P(None, 'tp')
- grad_w_value: float32 [768, 768], P(None, 'tp')
- grad_w_attn_out: float32 [768, 768], P('tp')
- grad_gain_attn: float32 [768], replicated
- grad_gain_moe: float32 [768], replicated
- grad_rel_bias: float32 [32, 12], P(None, 'tp')
- grad_w_router: float32 [768, 8], replicated
- grad_w_in: float32 [8, 768, 3072], P('ex', None, 'tp')
- grad_w_out: float32 [8, 3072, 768], P('ex', 'tp')
Inputs may be any that keep to these rules, and one draw needn't show every extreme that they name: `routes`: each row names two different experts. The rows of one index of ex name any one expert at most 64 times, a bound that some block reaches. `lengths`: each row sums to 128 and its largest entry is exactly 96.
All inputs are finite; a program needn't handle non-finite values.
Results may differ from a plain program's by a relative error of at most 0.017.
Values may be sent and summed in bfloat16 or wider, within the bound.
A program may use at most 128 MiB of HBM per device.

v0:
```python
from functools import partial
import math
import jax
import jax.numpy as jnp
from jax import lax
from jax.sharding import PartitionSpec as P

eps = 1e-06
highest = lax.Precision.HIGHEST
bucket_edges = [math.ceil(16 * 8 ** (number / 16)) for number in range(1, 16)]


def rms_scale(values):
    return lax.rsqrt(jnp.mean(values * values, -1, keepdims=True) + eps)


def bucket_of(length):
    positions = jnp.arange(length, dtype=jnp.int32)
    offsets = positions[:, None] - positions[None, :]
    distance = jnp.maximum(offsets, 0)
    counted = jnp.zeros_like(distance)
    for border in bucket_edges:
        counted = counted + (distance >= border).astype(jnp.int32)
    return jnp.where(distance < 16, distance, 16 + counted)


def contract_rows(left_side, right_side):
    return lax.dot_general(
        left_side, right_side, (((0,), (0,)), ((), ())), preferred_element_type=jnp.float32
    )


def contract_cols(left_side, right_side):
    return lax.dot_general(
        left_side, right_side, (((1,), (1,)), ((), ())), preferred_element_type=jnp.float32
    )


def shards(
    inputs,
    routes,
    lengths,
    w_query,
    w_key,
    w_value,
    w_attn_out,
    gain_attn,
    gain_moe,
    rel_bias,
    w_router,
    w_in,
    w_out,
    cotangent,
):
    tok_rows, model_width = inputs.shape
    local_heads = rel_bias.shape[1]
    head_dim = w_query.shape[1] // local_heads
    attn_scale = head_dim ** (-0.5)
    experts = w_router.shape[1]
    ex_devices = lax.axis_size("ex")
    local_experts = w_in.shape[0]
    capacity = 4 * tok_rows // experts
    pair_count = 2 * tok_rows
    inputs_f = inputs.astype(jnp.float32)
    scale_a = rms_scale(inputs_f)
    normed_a = inputs_f * scale_a
    attn_in = (normed_a * gain_attn).astype(jnp.bfloat16)
    query_b = (
        jnp.dot(attn_in, w_query, preferred_element_type=jnp.float32)
        .astype(jnp.bfloat16)
        .reshape(tok_rows, local_heads, head_dim)
    )
    key_b = (
        jnp.dot(attn_in, w_key, preferred_element_type=jnp.float32)
        .astype(jnp.bfloat16)
        .reshape(tok_rows, local_heads, head_dim)
    )
    value_b = (
        jnp.dot(attn_in, w_value, preferred_element_type=jnp.float32)
        .astype(jnp.bfloat16)
        .reshape(tok_rows, local_heads, head_dim)
    )
    buckets = bucket_of(tok_rows)
    one_hot = (
        buckets[None] == jnp.arange(rel_bias.shape[0], dtype=jnp.int32)[:, None, None]
    ).astype(jnp.float32)
    bias_full = jnp.einsum("bij,bh->hij", one_hot, rel_bias, precision=highest)
    seq_count = lengths.shape[1]
    seq_order = jnp.arange(seq_count, dtype=jnp.int32)
    seq_ends = jnp.sum(
        jnp.where(seq_order[None, :] <= seq_order[:, None], lengths[0][None, :], 0), -1
    )
    positions = jnp.arange(tok_rows, dtype=jnp.int32)
    segments = jnp.sum((positions[:, None] >= seq_ends[None, :]).astype(jnp.int32), -1)
    allowed = (segments[:, None] == segments[None, :]) & (positions[:, None] >= positions[None, :])

    def score_of(queries_in, keys_in):
        raw_scores = (
            jnp.einsum("ihd,jhd->hij", queries_in, keys_in, preferred_element_type=jnp.float32)
            * attn_scale
        )
        return jnp.where(allowed[None], raw_scores + bias_full, -1e30)

    scores = score_of(query_b, key_b)
    row_max = jnp.max(scores, -1, keepdims=True)
    log_sum = row_max + jnp.log(jnp.sum(jnp.exp(scores - row_max), -1, keepdims=True))
    probabilities = jnp.exp(scores - log_sum)
    probs_low = probabilities.astype(jnp.bfloat16)
    mixed_heads = (
        jnp.einsum("hij,jhd->ihd", probs_low, value_b, preferred_element_type=jnp.float32)
        .astype(jnp.bfloat16)
        .reshape(tok_rows, -1)
    )
    head_part = jnp.dot(mixed_heads, w_attn_out, preferred_element_type=jnp.float32)
    residual = inputs_f + lax.psum(head_part, "tp")
    scale_m = rms_scale(residual)
    normed_m = residual * scale_m
    moe_in = (normed_m * gain_moe).astype(jnp.bfloat16)
    logits = jnp.dot(moe_in, w_router, preferred_element_type=jnp.float32)
    expert_ids = jnp.arange(experts, dtype=jnp.int32)
    route_hot = (routes[:, :, None] == expert_ids[None, None, :]).astype(jnp.float32)
    chosen_logits = jnp.sum(route_hot * logits[:, None, :], -1)
    gate_max = jnp.max(chosen_logits, -1, keepdims=True)
    gate_exp = jnp.exp(chosen_logits - gate_max)
    gate_values = gate_exp / jnp.sum(gate_exp, -1, keepdims=True)
    pair_routes = routes.reshape(-1)
    pair_hot = (pair_routes[:, None] == expert_ids[None, :]).astype(jnp.int32)
    pair_order = jnp.arange(pair_count, dtype=jnp.int32)
    slot_index = jnp.sum(
        (
            (pair_routes[:, None] == pair_routes[None, :])
            & (pair_order[None, :] < pair_order[:, None])
        ).astype(jnp.int32),
        -1,
    )
    pair_slots = pair_routes * capacity + slot_index
    members = (
        jnp.full((experts * capacity,), pair_count, jnp.int32)
        .at[pair_slots]
        .set(jnp.arange(pair_count, dtype=jnp.int32))
    )
    padded = jnp.concatenate([moe_in, jnp.zeros((1, model_width), jnp.bfloat16)], 0)
    send_rows = padded[members // 2].reshape(experts, capacity, model_width)
    arrived = lax.all_to_all(send_rows, "ex", split_axis=0, concat_axis=0, tiled=True)
    slot_count = arrived.shape[1]
    grouped = arrived.reshape(ex_devices, local_experts, slot_count, model_width)
    pre_act = jnp.einsum("slcd,ldf->slcf", grouped, w_in, preferred_element_type=jnp.float32)
    act_low = jax.nn.gelu(pre_act, approximate=True).astype(jnp.bfloat16)
    partial_out = jnp.einsum("slcf,lfd->slcd", act_low, w_out, preferred_element_type=jnp.float32)
    partial_out = partial_out.reshape(ex_devices * local_experts, slot_count, model_width)
    owned_rows = lax.psum_scatter(
        partial_out.astype(jnp.bfloat16), "tp", scatter_dimension=2, tiled=True
    )
    returned = lax.all_to_all(owned_rows, "ex", split_axis=0, concat_axis=0, tiled=True)
    returned, kept_rows, kept_pre = (
        returned,
        arrived,
        pre_act.reshape(ex_devices * local_experts, slot_count, -1),
    )
    expert_out = lax.all_gather(returned, "tp", axis=2, tiled=True).reshape(
        experts * capacity, model_width
    )
    pair_out = expert_out[pair_slots].reshape(tok_rows, 2, model_width).astype(jnp.float32)
    result = residual + jnp.sum(gate_values[:, :, None] * pair_out, 1)
    output = result.astype(jnp.bfloat16)
    grad_out = cotangent.astype(jnp.float32)
    gate_grad = jnp.sum(grad_out[:, None, :] * pair_out, -1)
    logit_pair = gate_values * (gate_grad - jnp.sum(gate_values * gate_grad, -1, keepdims=True))
    logit_grads = jnp.sum(logit_pair[:, :, None] * route_hot, 1)
    grad_router = jnp.dot(moe_in.astype(jnp.float32).T, logit_grads, precision=highest)
    moe_grad = jnp.dot(logit_grads, w_router.astype(jnp.float32).T, precision=highest)
    pair_grads = (
        (gate_values[:, :, None] * grad_out[:, None, :])
        .astype(jnp.bfloat16)
        .reshape(pair_count, model_width)
    )
    padded_grads = jnp.concatenate([pair_grads, jnp.zeros((1, model_width), jnp.bfloat16)], 0)
    send_grad_rows = padded_grads[members].reshape(experts, capacity, model_width)
    arrived_grads = lax.all_to_all(send_grad_rows, "ex", split_axis=0, concat_axis=0, tiled=True)
    grad_group = arrived_grads.reshape(ex_devices, local_experts, capacity, model_width)
    act_grad = jnp.einsum("slcd,lfd->slcf", grad_group, w_out, preferred_element_type=jnp.float32)
    pre_keep = kept_pre.reshape(ex_devices, local_experts, capacity, -1)
    act_value, gelu_back = jax.vjp(partial(jax.nn.gelu, approximate=True), pre_keep)
    pre_grad = gelu_back(act_grad)[0].astype(jnp.bfloat16)
    act_low = act_value.astype(jnp.bfloat16)
    grad_w_out = jnp.einsum(
        "slcf,slcd->lfd", act_low, grad_group, preferred_element_type=jnp.float32
    )
    rows_group = kept_rows.reshape(ex_devices, local_experts, capacity, model_width)
    grad_w_in = jnp.einsum(
        "slcd,slcf->ldf", rows_group, pre_grad, preferred_element_type=jnp.float32
    )
    row_part = jnp.einsum("slcf,ldf->slcd", pre_grad, w_in, preferred_element_type=jnp.float32)
    row_part = row_part.reshape(ex_devices * local_experts, capacity, model_width)
    row_share = lax.psum_scatter(row_part, "tp", scatter_dimension=2, tiled=True).astype(
        jnp.bfloat16
    )
    row_back = lax.all_to_all(row_share, "ex", split_axis=0, concat_axis=0, tiled=True)
    row_full = lax.all_gather(row_back, "tp", axis=2, tiled=True).reshape(
        experts * capacity, model_width
    )
    moe_grad = moe_grad + jnp.sum(
        row_full[pair_slots].reshape(tok_rows, 2, model_width).astype(jnp.float32), 1
    )
    grad_gain_moe = jnp.sum(moe_grad * normed_m, 0)
    normed_grad_m = moe_grad * gain_moe
    resid_grad = grad_out + scale_m * (
        normed_grad_m - normed_m * jnp.mean(normed_grad_m * normed_m, -1, keepdims=True)
    )
    attn_grad = resid_grad.astype(jnp.bfloat16)
    grad_w_attn_out = contract_rows(mixed_heads, attn_grad)
    mixed_grad = (
        contract_cols(attn_grad, w_attn_out)
        .astype(jnp.bfloat16)
        .reshape(tok_rows, local_heads, head_dim)
    )
    scores_again = score_of(query_b, key_b)
    probs_again = jnp.exp(scores_again - log_sum)
    prob_grad = jnp.einsum("ihd,jhd->hij", mixed_grad, value_b, preferred_element_type=jnp.float32)
    value_grad = jnp.einsum(
        "hij,ihd->jhd",
        probs_again.astype(jnp.bfloat16),
        mixed_grad,
        preferred_element_type=jnp.float32,
    ).astype(jnp.bfloat16)
    score_grad = probs_again * (prob_grad - jnp.sum(probs_again * prob_grad, -1, keepdims=True))
    grad_rel_bias = jnp.einsum("hij,bij->bh", score_grad, one_hot, precision=highest)
    score_low = score_grad.astype(jnp.bfloat16)
    query_grad = (
        (
            jnp.einsum("hij,jhd->ihd", score_low, key_b, preferred_element_type=jnp.float32)
            * attn_scale
        )
        .astype(jnp.bfloat16)
        .reshape(tok_rows, -1)
    )
    key_grad = (
        (
            jnp.einsum("hij,ihd->jhd", score_low, query_b, preferred_element_type=jnp.float32)
            * attn_scale
        )
        .astype(jnp.bfloat16)
        .reshape(tok_rows, -1)
    )
    value_flat = value_grad.reshape(tok_rows, -1)
    grad_w_query = contract_rows(attn_in, query_grad)
    grad_w_key = contract_rows(attn_in, key_grad)
    grad_w_value = contract_rows(attn_in, value_flat)
    input_part = (
        contract_cols(query_grad, w_query)
        + contract_cols(key_grad, w_key)
        + contract_cols(value_flat, w_value)
    )
    input_grad = lax.psum(input_part.astype(jnp.bfloat16), "tp").astype(jnp.float32)
    grad_gain_attn = jnp.sum(input_grad * normed_a, 0)
    normed_grad_a = input_grad * gain_attn
    grad_inputs = (
        resid_grad
        + scale_a
        * (normed_grad_a - normed_a * jnp.mean(normed_grad_a * normed_a, -1, keepdims=True))
    ).astype(jnp.bfloat16)
    dense_sums = lax.psum(
        (
            grad_w_query,
            grad_w_key,
            grad_w_value,
            grad_w_attn_out,
            grad_gain_attn,
            grad_gain_moe,
            grad_rel_bias,
            grad_router,
        ),
        "ex",
    )
    return (
        output,
        grad_inputs,
        dense_sums[0],
        dense_sums[1],
        dense_sums[2],
        dense_sums[3],
        dense_sums[4],
        dense_sums[5],
        dense_sums[6],
        dense_sums[7],
        grad_w_in,
        grad_w_out,
    )


def solution(mesh):
    placed = (
        P("ex", None),
        P("ex", None),
        P("ex", None),
        P(None, "tp"),
        P(None, "tp"),
        P(None, "tp"),
        P("tp", None),
        P(),
        P(),
        P(None, "tp"),
        P(),
        P("ex", None, "tp"),
        P("ex", "tp", None),
        P("ex", None),
    )
    return jax.shard_map(
        shards,
        mesh=mesh,
        in_specs=placed,
        out_specs=(
            P("ex", None),
            P("ex", None),
            P(None, "tp"),
            P(None, "tp"),
            P(None, "tp"),
            P("tp", None),
            P(),
            P(),
            P(None, "tp"),
            P(),
            P("ex", None, "tp"),
            P("ex", "tp", None),
        ),
        check_vma=False,
    )
```

profile of v0, /device:TPU:0, one launch (start us, length us, event | category | flops | bytes accessed | tf_op | source)
XLA Modules:
  0.0 362.4 jit_solution(8996711575034821394)
XLA Ops:
  17.6 32.7 %all-reduce.8.cloned.1.call-done = f32[128,768]{1,0:T(8,128)} async-done(((f32[128,768]{1,0:T(8,128)}), f32[128,768]{1,0:T(8,128)}) %all-reduce.8.cloned.1.call-update) | async-done | bytes 393232 | tf_op jit(solution)/shard_map/psum | solution.py:115
  52.8 2.7 gather_fusion
  55.5 5.6 %all-to-all-start = ((bf16[8,64,768]{2,1,0:T(8,128)(2,1)}), bf16[8,64,768]{2,1,0:T(8,128)(2,1)}, u32[]{:S(2)}, u32[]{:S(2)}) async-start(bf16[8,64,768]{2,1,0:T(8,128)(2,1)} %bitcast.10), calls=%async_computation | async-start | bytes 1572864 | tf_op jit(solution)/shard_map/all_to_all | solution.py:144
  65.3 2.7 gather_fusion.2
  68.0 12.4 %all-to-all-done = bf16[8,64,768]{2,1,0:T(8,128)(2,1)} async-done(((bf16[8,64,768]{2,1,0:T(8,128)(2,1)}), bf16[8,64,768]{2,1,0:T(8,128)(2,1)}, u32[]{:S(2)}, u32[]{:S(2)}) %all-to-all-start) | async-done | bytes 786464 | tf_op jit(solution)/shard_map/all_to_all | solution.py:144
  80.4 4.4 %all-to-all-start.2 = ((bf16[8,64,768]{2,1,0:T(8,128)(2,1)}), bf16[8,64,768]{2,1,0:T(8,128)(2,1)}, u32[]{:S(2)}, u32[]{:S(2)}) async-start(bf16[8,64,768]{2,1,0:T(8,128)(2,1)} %bitcast.22), calls=%async_computation.2 | async-start | bytes 1572864 | tf_op jit(solution)/shard_map/all_to_all | solution.py:179
  84.9 1.9 fusion.18
  87.9 2.0 convolution_convert_fusion
  89.9 2.0 copy.92
  93.8 10.5 %all-to-all-done.2 = bf16[8,64,768]{2,1,0:T(8,128)(2,1)} async-done(((bf16[8,64,768]{2,1,0:T(8,128)(2,1)}), bf16[8,64,768]{2,1,0:T(8,128)(2,1)}, u32[]{:S(2)}, u32[]{:S(2)}) %all-to-all-start.2) | async-done | bytes 786464 | tf_op jit(solution)/shard_map/all_to_all | solution.py:179
  104.3 3.1 fusion.13
  108.3 2.1 fusion.16
  110.4 2.3 copy.94
  112.7 3.7 %reshape.446 = f32[768,512]{1,0:T(8,128)} reshape(f32[768,8,64]{2,1,0:T(8,128)} %bitcast.142) | data formatting | bytes 3145728
  120.1 5.5 %all-to-all-start.1 = ((bf16[8,64,192]{2,1,0:T(8,128)(2,1)}), bf16[8,64,192]{2,1,0:T(8,128)(2,1)S(1)}, u32[]{:S(2)}, u32[]{:S(2)}) async-start(bf16[8,64,192]{2,1,0:T(8,128)(2,1)} %copy.93), calls=%async_computation.1 | async-start | bytes 524288 | tf_op jit(solution)/shard_map/all_to_all | solution.py:154
  126.4 8.1 %all-to-all-done.1 = bf16[8,64,192]{2,1,0:T(8,128)(2,1)S(1)} async-done(((bf16[8,64,192]{2,1,0:T(8,128)(2,1)}), bf16[8,64,192]{2,1,0:T(8,128)(2,1)S(1)}, u32[]{:S(2)}, u32[]{:S(2)}) %all-to-all-start.1) | async-done | bytes 196640 | tf_op jit(solution)/shard_map/all_to_all | solution.py:154
  134.8 20.2 %all_gather.6 = bf16[8,64,768]{1,0,2:T(8,128)(2,1)} all-gather(bf16[8,64,192]{1,0,2:T(8,128)(2,1)S(1)} %copy.77), channel_id=1, replica_groups=mesh['ex'=8,'tp'=4] {'tp'}, dimensions={2}, use_global_device_ids=true | all-gather | bytes 983040 | tf_op jit(solution)/shard_map/all_gather | solution.py:160
  154.9 2.0 copy.78
  158.6 2.4 multiply_reduce_fusion
  163.3 3.4 all-to-all-start.3
  166.8 9.5 %all-to-all-done.3 = bf16[8,64,192]{2,1,0:T(8,128)(2,1)S(1)} async-done(((bf16[8,64,192]{2,1,0:T(8,128)(2,1)}), bf16[8,64,192]{2,1,0:T(8,128)(2,1)S(1)}, u32[]{:S(2)}, u32[]{:S(2)}) %all-to-all-start.3) | async-done | bytes 196640 | tf_op jit(solution)/shard_map/all_to_all | solution.py:198
  176.6 13.6 %all_gather.7 = bf16[8,64,768]{1,0,2:T(8,128)(2,1)} all-gather(bf16[8,64,192]{1,0,2:T(8,128)(2,1)S(1)} %copy.82), channel_id=1, replica_groups=mesh['ex'=8,'tp'=4] {'tp'}, dimensions={2}, use_global_device_ids=true | all-gather | bytes 983040 | tf_op jit(solution)/shard_map/all_gather | solution.py:199
  190.2 2.0 copy.83
  192.2 1.9 gather_fusion.3
  195.5 1.7 reduce_sum.177
  206.7 3.5 convolution_bitcast_fusion.1
  210.2 3.5 convolution_bitcast_fusion
  215.2 21.0 %all-reduce.10.cloned.1.call-done = bf16[128,768]{1,0:T(8,128)(2,1)} async-done(((bf16[128,768]{1,0:T(8,128)(2,1)}), bf16[128,768]{1,0:T(8,128)(2,1)}) %all-reduce.10.cloned.1.call-update) | async-done | bytes 196624 | tf_op jit(solution)/shard_map/psum | solution.py:254
  237.4 40.2 %all-reduce.2 = (f32[768]{0:T(1024)}, f32[768]{0:T(1024)}, f32[32,3]{0,1:T(4,128)}, f32[768,8]{0,1:T(8,128)}) all-reduce(f32[768]{0:T(1024)S(1)} %get-tuple-element.16, f32[768]{0:T(1024)S(1)} %get-tuple-element.12, f32[32,3]{0,1:T(4,128)S(1)} %fusion.25, f32[768,8]{0,1:T(8,128)S(1)} %fusion.97), channel_id=1, replica_groups=mesh['ex'=8,'tp'=4] {'ex'}, use_global_device_ids=true, to_apply=%region_28.29 | all-reduce | flops 7776 | bytes 62208 | tf_op jit(solution)/shard_map/psum | solution.py:262
  277.6 1.8 fusion.37
  279.4 72.0 %all-reduce.12.cloned.1.call-done = (f32[768,192]{0,1:T(8,128)}, f32[768,192]{0,1:T(8,128)}, f32[768,192]{0,1:T(8,128)}, f32[192,768]{1,0:T(8,128)}) async-done(((f32[768,192]{0,1:T(8,128)}, f32[768,192]{0,1:T(8,128)}, f32[768,192]{0,1:T(8,128)}, f32[192,768]{1,0:T(8,128)}), (f32[768,192]{0,1:T(8,128)}, f32[768,192]{0,1:T(8,128)}, f32[768,192]{0,1:T(8,128)}, ...) | async-done | bytes 2359312 | tf_op jit(solution)/shard_map/psum | solution.py:262
  351.4 2.0 copy.102
  (194 shorter events, 45.2 us)
Async XLA Ops:
  7.2 80.7 %copy-start = (bf16[1,768,768]{2,1,0:T(8,128)(2,1)S(1)}, bf16[1,768,768]{2,1,0:T(8,128)(2,1)}, u32[]{:S(2)}) copy-start(bf16[1,768,768]{2,1,0:T(8,128)(2,1)} %param.26) | copy-start | bytes 3538948
  7.2 4.5 %copy-start.1 = (bf16[128,768]{1,0:T(8,128)(2,1)S(1)}, bf16[128,768]{1,0:T(8,128)(2,1)}, u32[]{:S(2)}) copy-start(bf16[128,768]{1,0:T(8,128)(2,1)} %param.14) | copy-start | bytes 589828
  7.2 4.5 %copy-start.26 = (f32[768]{0:T(1024)S(1)}, f32[768]{0:T(1024)}, u32[]{:S(2)}) copy-start(f32[768]{0:T(1024)} %param.21) | copy-start | bytes 9220
  7.2 4.5 %copy-start.16 = (bf16[768,192]{0,1:T(8,128)(2,1)S(1)}, bf16[768,192]{0,1:T(8,128)(2,1)}, u32[]{:S(2)}) copy-start(bf16[768,192]{0,1:T(8,128)(2,1)} %param.17) | copy-start | bytes 884740
  7.2 4.8 %copy-start.18 = (bf16[768,192]{0,1:T(8,128)(2,1)S(1)}, bf16[768,192]{0,1:T(8,128)(2,1)}, u32[]{:S(2)}) copy-start(bf16[768,192]{0,1:T(8,128)(2,1)} %param.18) | copy-start | bytes 884740
  7.2 5.1 %copy-start.45 = (s32[1,4]{1,0:T(1,128)S(1)}, s32[1,4]{1,0:T(1,128)}, u32[]{:S(2)}) copy-start(s32[1,4]{1,0:T(1,128)} %param.16) | copy-start | bytes 52
  7.3 43.1 %all-reduce.8.cloned.1.call-start = ((), (), s32[]{:S(2)}) async-start(), calls=%async_computation.6 | async-start | bytes 786432 | tf_op jit(solution)/shard_map/psum | solution.py:115
  7.4 5.3 %copy-start.27 = (s32[128,128]{1,0:T(8,128)}, s32[128,128]{1,0:T(8,128)S(1)}, u32[]{:S(2)}) copy-start(s32[128,128]{1,0:T(8,128)S(1)} %compare_select_fusion) | copy-start | bytes 196612
  8.7 4.0 %copy-start.35 = (f32[128]{0:T(128)}, f32[128]{0:T(128)S(1)}, u32[]{:S(2)}) copy-start(f32[128]{0:T(128)S(1)} %add_rsqrt_fusion.1) | copy-start | bytes 1540
  10.1 3.8 %copy-start.6 = (bf16[192,768]{1,0:T(8,128)(2,1)S(1)}, bf16[192,768]{1,0:T(8,128)(2,1)}, u32[]{:S(2)}) copy-start(bf16[192,768]{1,0:T(8,128)(2,1)} %param.20) | copy-start | bytes 884740
  12.4 39.1 %copy-start.22 = (bf16[128,192]{0,1:T(8,128)(2,1)}, bf16[128,192]{0,1:T(8,128)(2,1)S(1)}, u32[]{:S(2)}) copy-start(bf16[128,192]{0,1:T(8,128)(2,1)S(1)} %convolution_convert_fusion.4) | copy-start | bytes 147460
  13.0 39.0 %copy-start.30 = (f32[768]{0:T(1024)S(1)}, f32[768]{0:T(1024)}, u32[]{:S(2)}) copy-start(f32[768]{0:T(1024)} %param.22) | copy-start | bytes 9220
  55.5 5.6 %copy-start.4 = (bf16[128,768]{1,0:T(8,128)(2,1)S(1)}, bf16[128,768]{1,0:T(8,128)(2,1)}, u32[]{:S(2)}) copy-start(bf16[128,768]{1,0:T(8,128)(2,1)} %param.27) | copy-start | bytes 589828
  55.5 24.9 %all-to-all-start = ((bf16[8,64,768]{2,1,0:T(8,128)(2,1)}), bf16[8,64,768]{2,1,0:T(8,128)(2,1)}, u32[]{:S(2)}, u32[]{:S(2)}) async-start(bf16[8,64,768]{2,1,0:T(8,128)(2,1)} %bitcast.10), calls=%async_computation | async-start | bytes 1572864 | tf_op jit(solution)/shard_map/all_to_all | solution.py:144
  80.4 4.4 %copy-start.44 = (bf16[1,768,768]{2,1,0:T(8,128)(2,1)S(1)}, bf16[1,768,768]{2,1,0:T(8,128)(2,1)}, u32[]{:S(2)}) copy-start(bf16[1,768,768]{2,1,0:T(8,128)(2,1)} %param.25) | copy-start | bytes 3538948
  80.4 23.9 %all-to-all-start.2 = ((bf16[8,64,768]{2,1,0:T(8,128)(2,1)}), bf16[8,64,768]{2,1,0:T(8,128)(2,1)}, u32[]{:S(2)}, u32[]{:S(2)}) async-start(bf16[8,64,768]{2,1,0:T(8,128)(2,1)} %bitcast.22), calls=%async_computation.2 | async-start | bytes 1572864 | tf_op jit(solution)/shard_map/all_to_all | solution.py:179
  84.8 33.1 %reduce-scatter.7.cloned.1.call-start = ((), (), s32[]{:S(2)}) async-start(), calls=%async_computation.8 | async-start | bytes 983040
  93.6 67.4 %reduce-scatter.9.cloned.1.call-start = ((), (), s32[]{:S(2)}) async-start(), calls=%async_computation.9 | async-start | bytes 1966080
  116.4 9.2 %copy-start.5 = (bf16[128,768]{1,0:T(8,128)(2,1)S(1)}, bf16[128,768]{1,0:T(8,128)(2,1)}, u32[]{:S(2)}) copy-start(bf16[128,768]{1,0:T(8,128)(2,1)} %param.27) | copy-start | bytes 589828
  116.5 9.9 %copy-start.43 = (s32[256,1]{0,1:T(1,128)S(1)}, s32[256,1]{0,1:T(1,128)}, u32[]{:S(2)}) copy-start(s32[256,1]{0,1:T(1,128)} %copy-done.42) | copy-start | bytes 3076
  120.1 14.4 %all-to-all-start.1 = ((bf16[8,64,192]{2,1,0:T(8,128)(2,1)}), bf16[8,64,192]{2,1,0:T(8,128)(2,1)S(1)}, u32[]{:S(2)}, u32[]{:S(2)}) async-start(bf16[8,64,192]{2,1,0:T(8,128)(2,1)} %copy.93), calls=%async_computation.1 | async-start | bytes 524288 | tf_op jit(solution)/shard_map/all_to_all | solution.py:154
  158.5 8.2 %copy-start.34 = (f32[128]{0:T(128)S(1)}, f32[128]{0:T(128)}, u32[]{:S(2)}) copy-start(f32[128]{0:T(128)} %copy-done.33) | copy-start | bytes 1540
  158.6 8.2 %copy-start.39 = (f32[128]{0:T(128)S(1)}, f32[128]{0:T(128)}, u32[]{:S(2)}) copy-start(f32[128]{0:T(128)} %copy-done.38) | copy-start | bytes 1540
  158.6 8.2 %copy-start.32 = (s32[128,2]{0,1:T(2,128)S(1)}, s32[128,2]{0,1:T(2,128)}, u32[]{:S(2)}) copy-start(s32[128,2]{0,1:T(2,128)} %param.15) | copy-start | bytes 3076
  163.3 13.1 %all-to-all-start.3 = ((bf16[8,64,192]{2,1,0:T(8,128)(2,1)}), bf16[8,64,192]{2,1,0:T(8,128)(2,1)S(1)}, u32[]{:S(2)}, u32[]{:S(2)}) async-start(bf16[8,64,192]{2,1,0:T(8,128)(2,1)} %copy.95), calls=%async_computation.3 | async-start | bytes 524288 | tf_op jit(solution)/shard_map/all_to_all | solution.py:198
  166.7 69.5 %all-reduce.10.cloned.1.call-start = ((), (), s32[]{:S(2)}) async-start(), calls=%async_computation.7 | async-start | bytes 393216 | tf_op jit(solution)/shard_map/psum | solution.py:254
  200.8 3.5 copy-start.19
  205.5 145.8 %all-reduce.12.cloned.1.call-start = ((), (), s32[]{:S(2)}) async-start(), calls=%async_computation.10 | async-start | bytes 4718592 | tf_op jit(solution)/shard_map/psum | solution.py:262
  206.7 3.5 copy-start.47
  210.2 3.5 copy-start.3
  210.2 3.9 %copy-start.28 = (s32[128,128]{1,0:T(8,128)S(1)}, s32[128,128]{1,0:T(8,128)}, u32[]{:S(2)}) copy-start(s32[128,128]{1,0:T(8,128)} %copy-done.27) | copy-start | bytes 196612
  351.4 3.7 %copy-start.8 = (f32[192,768]{1,0:T(8,128)S(1)}, f32[192,768]{1,0:T(8,128)}, u32[]{:S(2)}) copy-start(f32[192,768]{1,0:T(8,128)} %get-tuple-element.44) | copy-start | bytes 1769476
  (27 other events, 46.2 us)
Sparse Core Ops, SparseCore 0:
  15.0 35.3 all-reduce.7
  93.7 24.1 reduce-scatter.6
  121.0 34.1 reduce-scatter.8
  205.6 30.4 all-reduce.9
  240.5 110.7 all-reduce.11
where the time goes:
time: 364 us; the launch traced here: 362 us
  waiting for transfers between devices  168 us (46%)
  blocking collectives  74 us (20%)
  local copies, waits for them, and re-layouts  41.8 us (11%)
  matrix products  31.6 us (9%)
  starting transfers between devices  19.3 us (5%)
  between operations  14.6 us (4%)
  other arithmetic  13.4 us (4%)
    psum x1, waiting for transfers between devices, shards(): lax.psum((grad_w_query, grad_w_key, grad_w_value, grad_w_attn_out, grad_g...  72 us
    psum x1, blocking collectives, shards(): lax.psum((grad_w_query, grad_w_key, grad_w_value, grad_w_attn_out, grad_g...  40.2 us
    psum x1, waiting for transfers between devices, shards(): residual = inputs_f + lax.psum(head_part, 'tp')  32.7 us
    unnamed x113, local copies, waits for them, and re-layouts  23.8 us
    psum x1, waiting for transfers between devices, shards(): lax.psum(input_part.astype(jnp.bfloat16), 'tp').astype(jnp.float32)  21 us
    all_gather x1, blocking collectives, shards(): lax.all_gather(returned, 'tp', axis=2, tiled=True)  20.2 us
    all_gather x1, blocking collectives, shards(): lax.all_gather(row_back, 'tp', axis=2, tiled=True)  13.6 us
    all_to_all x1, waiting for transfers between devices, shards(): lax.all_to_all(send_rows, 'ex', split_axis=0, concat_axis=0, tiled=True)  12.4 us
  transfers between devices with their start and end apart: 9, of which 8 were waited for; matrix products, arithmetic and copies ran while one was open for 14% of the time, Pallas kernels for 0%

commit v1 on v0

--- a/solution.py
+++ b/solution.py
@@ -8,6 +8,11 @@
 eps = 1e-06
 highest = lax.Precision.HIGHEST
 bucket_edges = [math.ceil(16 * 8 ** (number / 16)) for number in range(1, 16)]
+
+
+def summed_here(array, axis):
+    pieces = lax.all_gather(array, axis)
+    return jnp.sum(pieces, axis=0)
 
 
 def rms_scale(values):
@@ -251,7 +256,7 @@
         + contract_cols(key_grad, w_key)
         + contract_cols(value_flat, w_value)
     )
-    input_grad = lax.psum(input_part.astype(jnp.bfloat16), "tp").astype(jnp.float32)
+    input_grad = summed_here(input_part.astype(jnp.bfloat16), "tp").astype(jnp.float32)
     grad_gain_attn = jnp.sum(input_grad * normed_a, 0)
     normed_grad_a = input_grad * gain_attn
     grad_inputs = (

time: 364 us -> 328 us (0.901)
  waiting for transfers between devices: 168 us -> 126 us
  blocking collectives: 74 us -> 80.6 us
    psum x1 -> x0, waiting for transfers between devices: 21 us -> none  [shards(): lax.psum(input_part.astype(jnp.bfloat16), 'tp').astype(jnp.float32)]
    psum x1, waiting for transfers between devices: 72 us -> 56.1 us  [shards(): lax.psum((grad_w_query, grad_w_key, grad_w_value, grad_w_attn_out, grad_g...]
    all_gather x0 -> x1, blocking collectives: none -> 8.74 us  [summed_here(): pieces = lax.all_gather(array, axis)]
    unnamed x113 -> x109, local copies, waits for them, and re-layouts: 23.8 us -> 25.2 us
  transfers between devices with their start and end apart: 9 -> 8, of which waited for: 8 -> 6; matrix products, arithmetic and copies ran while one was open for 14% -> 15% of each run, Pallas kernels for 0% -> 0%
where the time goes in v1:
time: 328 us; the launch traced here: 327 us
  waiting for transfers between devices  126 us (38%)
  blocking collectives  80.6 us (25%)
  local copies, waits for them, and re-layouts  43.2 us (13%)
  matrix products  31.5 us (10%)
  starting transfers between devices  18.9 us (6%)
  between operations  14.6 us (4%)
  other arithmetic  11.7 us (4%)
    psum x1, waiting for transfers between devices, shards(): lax.psum((grad_w_query, grad_w_key, grad_w_value, grad_w_attn_out, grad_g...  56.1 us
    psum x1, blocking collectives, shards(): lax.psum((grad_w_query, grad_w_key, grad_w_value, grad_w_attn_out, grad_g...  37.5 us
    psum x1, waiting for transfers between devices, shards(): residual = inputs_f + lax.psum(head_part, 'tp')  32.7 us
    unnamed x109, local copies, waits for them, and re-layouts  25.2 us
    all_gather x1, blocking collectives, shards(): lax.all_gather(returned, 'tp', axis=2, tiled=True)  20.7 us
    all_gather x1, blocking collectives, shards(): lax.all_gather(row_back, 'tp', axis=2, tiled=True)  13.7 us
    all_to_all x1, waiting for transfers between devices, shards(): lax.all_to_all(send_rows, 'ex', split_axis=0, concat_axis=0, tiled=True)  12.4 us
    all_to_all x1, waiting for transfers between devices, shards(): lax.all_to_all(send_grad_rows, 'ex', split_axis=0, concat_axis=0, tiled=T...  10.5 us
  transfers between devices with their start and end apart: 8, of which 6 were waited for; matrix products, arithmetic and copies ran while one was open for 15% of the time, Pallas kernels for 0%

profile of v1, /device:TPU:0, one launch (start us, length us, event | category | flops | bytes accessed | tf_op | source)
XLA Modules:
  0.0 326.7 jit_solution(12547431043709358117)
XLA Ops:
  17.6 32.7 %all-reduce.7.cloned.1.call-done = f32[128,768]{1,0:T(8,128)} async-done(((f32[128,768]{1,0:T(8,128)}), f32[128,768]{1,0:T(8,128)}) %all-reduce.7.cloned.1.call-update) | async-done | bytes 393232 | tf_op jit(solution)/shard_map/psum | solution.py:120
  52.8 2.7 gather_fusion
  55.5 5.6 %all-to-all-start = ((bf16[8,64,768]{2,1,0:T(8,128)(2,1)}), bf16[8,64,768]{2,1,0:T(8,128)(2,1)}, u32[]{:S(2)}, u32[]{:S(2)}) async-start(bf16[8,64,768]{2,1,0:T(8,128)(2,1)} %bitcast.10), calls=%async_computation | async-start | bytes 1572864 | tf_op jit(solution)/shard_map/all_to_all | solution.py:149
  65.3 2.7 gather_fusion.2
  68.1 12.4 %all-to-all-done = bf16[8,64,768]{2,1,0:T(8,128)(2,1)} async-done(((bf16[8,64,768]{2,1,0:T(8,128)(2,1)}), bf16[8,64,768]{2,1,0:T(8,128)(2,1)}, u32[]{:S(2)}, u32[]{:S(2)}) %all-to-all-start) | async-done | bytes 786464 | tf_op jit(solution)/shard_map/all_to_all | solution.py:149
  80.4 4.3 %all-to-all-start.2 = ((bf16[8,64,768]{2,1,0:T(8,128)(2,1)}), bf16[8,64,768]{2,1,0:T(8,128)(2,1)}, u32[]{:S(2)}, u32[]{:S(2)}) async-start(bf16[8,64,768]{2,1,0:T(8,128)(2,1)} %bitcast.22), calls=%async_computation.2 | async-start | bytes 1572864 | tf_op jit(solution)/shard_map/all_to_all | solution.py:184
  84.8 1.9 fusion.18
  87.9 1.9 convolution_convert_fusion
  89.9 2.0 copy.92
  91.9 1.7 reshape.445
  93.8 10.5 %all-to-all-done.2 = bf16[8,64,768]{2,1,0:T(8,128)(2,1)} async-done(((bf16[8,64,768]{2,1,0:T(8,128)(2,1)}), bf16[8,64,768]{2,1,0:T(8,128)(2,1)}, u32[]{:S(2)}, u32[]{:S(2)}) %all-to-all-start.2) | async-done | bytes 786464 | tf_op jit(solution)/shard_map/all_to_all | solution.py:184
  104.3 3.1 fusion.13
  108.4 2.1 fusion.16
  110.5 2.3 copy.94
  112.8 3.7 %reshape.447 = f32[768,512]{1,0:T(8,128)} reshape(f32[768,8,64]{2,1,0:T(8,128)} %bitcast.143) | data formatting | bytes 3145728
  120.4 5.2 %all-to-all-start.1 = ((bf16[8,64,192]{2,1,0:T(8,128)(2,1)}), bf16[8,64,192]{2,1,0:T(8,128)(2,1)S(1)}, u32[]{:S(2)}, u32[]{:S(2)}) async-start(bf16[8,64,192]{2,1,0:T(8,128)(2,1)} %copy.93), calls=%async_computation.1 | async-start | bytes 524288 | tf_op jit(solution)/shard_map/all_to_all | solution.py:159
  125.6 4.0 %convolution_bitcast_fusion = f32[1,768,768]{2,1,0:T(8,128)} fusion(bf16[8,64,768]{2,1,0:T(8,128)(2,1)} %all-to-all-done.2, f32[8,64,768]{2,1,0:T(8,128)} %copy-done.46), kind=kOutput, calls=%fused_computation.10 | convolution fusion | flops 607518720 | bytes 4718592 | tf_op jit(solution)/shard_map/slcf,slcd->lfd/dot_general | solution.py:191
  129.5 5.0 %all-to-all-done.1 = bf16[8,64,192]{2,1,0:T(8,128)(2,1)S(1)} async-done(((bf16[8,64,192]{2,1,0:T(8,128)(2,1)}), bf16[8,64,192]{2,1,0:T(8,128)(2,1)S(1)}, u32[]{:S(2)}, u32[]{:S(2)}) %all-to-all-start.1) | async-done | bytes 196640 | tf_op jit(solution)/shard_map/all_to_all | solution.py:159
  134.7 20.7 %all_gather.12 = bf16[8,64,768]{1,0,2:T(8,128)(2,1)} all-gather(bf16[8,64,192]{1,0,2:T(8,128)(2,1)S(1)} %copy.77), channel_id=1, replica_groups=mesh['ex'=8,'tp'=4] {'tp'}, dimensions={2}, use_global_device_ids=true | all-gather | bytes 983040 | tf_op jit(solution)/shard_map/all_gather | solution.py:165
  155.4 2.0 copy.78
  159.1 2.4 multiply_reduce_fusion
  163.7 3.4 %all-to-all-start.3 = ((bf16[8,64,192]{2,1,0:T(8,128)(2,1)}), bf16[8,64,192]{2,1,0:T(8,128)(2,1)S(1)}, u32[]{:S(2)}, u32[]{:S(2)}) async-start(bf16[8,64,192]{2,1,0:T(8,128)(2,1)} %copy.95), calls=%async_computation.3 | async-start | bytes 524288 | tf_op jit(solution)/shard_map/all_to_all | solution.py:203
  167.3 9.5 %all-to-all-done.3 = bf16[8,64,192]{2,1,0:T(8,128)(2,1)S(1)} async-done(((bf16[8,64,192]{2,1,0:T(8,128)(2,1)}), bf16[8,64,192]{2,1,0:T(8,128)(2,1)S(1)}, u32[]{:S(2)}, u32[]{:S(2)}) %all-to-all-start.3) | async-done | bytes 196640 | tf_op jit(solution)/shard_map/all_to_all | solution.py:203
  177.1 13.7 %all_gather.13 = bf16[8,64,768]{1,0,2:T(8,128)(2,1)} all-gather(bf16[8,64,192]{1,0,2:T(8,128)(2,1)S(1)} %copy.82), channel_id=1, replica_groups=mesh['ex'=8,'tp'=4] {'tp'}, dimensions={2}, use_global_device_ids=true | all-gather | bytes 983040 | tf_op jit(solution)/shard_map/all_gather | solution.py:204
  190.7 2.0 copy.83
  192.8 1.9 gather_fusion.3
  196.1 1.7 reduce_sum.189
  205.8 3.6 %convolution_bitcast_fusion.1 = f32[1,768,768]{2,1,0:T(8,128)} fusion(bf16[8,64,768]{2,1,0:T(8,128)(2,1)} %all-to-all-done, bf16[8,64,768]{2,1,0:T(8,128)(2,1)} %copy-done.47), kind=kOutput, calls=%fused_computation.11 | convolution fusion | flops 603979776 | bytes 3932160 | tf_op jit(solution)/shard_map/slcd,slcf->ldf/dot_general | solution.py:195
  211.0 8.7 %all-gather = bf16[512,768]{1,0:T(8,128)(2,1)S(1)} all-gather(bf16[128,768]{1,0:T(8,128)(2,1)S(1)} %fusion.20), channel_id=2, replica_groups=mesh['ex'=8,'tp'=4] {'tp'}, dimensions={0}, use_global_device_ids=true | all-gather | bytes 983040 | tf_op jit(solution)/shard_map/all_gather | solution.py:14
  221.2 37.5 %all-reduce.2 = (f32[768]{0:T(1024)}, f32[768]{0:T(1024)}, f32[32,3]{0,1:T(4,128)}, f32[768,8]{0,1:T(8,128)}) all-reduce(f32[768]{0:T(1024)S(1)} %get-tuple-element.16, f32[768]{0:T(1024)S(1)} %get-tuple-element.12, f32[32,3]{0,1:T(4,128)S(1)} %fusion.25, f32[768,8]{0,1:T(8,128)S(1)} %fusion.97), channel_id=1, replica_groups=mesh['ex'=8,'tp'=4] {'ex'}, use_global_device_ids=true, to_apply=%region_28.29 | all-reduce | flops 7776 | bytes 62208 | tf_op jit(solution)/shard_map/psum | solution.py:267
  259.5 56.1 %all-reduce.9.cloned.1.call-done = (f32[768,192]{0,1:T(8,128)}, f32[768,192]{0,1:T(8,128)}, f32[768,192]{0,1:T(8,128)}, f32[192,768]{1,0:T(8,128)}) async-done(((f32[768,192]{0,1:T(8,128)}, f32[768,192]{0,1:T(8,128)}, f32[768,192]{0,1:T(8,128)}, f32[192,768]{1,0:T(8,128)}), (f32[768,192]{0,1:T(8,128)}, f32[768,192]{0,1:T(8,128)}, f32[768,192]{0,1:T(8,128)}, ...) | async-done | bytes 2359312 | tf_op jit(solution)/shard_map/psum | solution.py:267
  315.7 2.0 copy.101
  (189 shorter events, 42.9 us)
Async XLA Ops:
  7.2 80.7 %copy-start = (bf16[1,768,768]{2,1,0:T(8,128)(2,1)S(1)}, bf16[1,768,768]{2,1,0:T(8,128)(2,1)}, u32[]{:S(2)}) copy-start(bf16[1,768,768]{2,1,0:T(8,128)(2,1)} %param.26) | copy-start | bytes 3538948
  7.2 4.5 %copy-start.1 = (bf16[128,768]{1,0:T(8,128)(2,1)S(1)}, bf16[128,768]{1,0:T(8,128)(2,1)}, u32[]{:S(2)}) copy-start(bf16[128,768]{1,0:T(8,128)(2,1)} %param.14) | copy-start | bytes 589828
  7.2 4.5 %copy-start.26 = (f32[768]{0:T(1024)S(1)}, f32[768]{0:T(1024)}, u32[]{:S(2)}) copy-start(f32[768]{0:T(1024)} %param.21) | copy-start | bytes 9220
  7.2 4.5 %copy-start.16 = (bf16[768,192]{0,1:T(8,128)(2,1)S(1)}, bf16[768,192]{0,1:T(8,128)(2,1)}, u32[]{:S(2)}) copy-start(bf16[768,192]{0,1:T(8,128)(2,1)} %param.17) | copy-start | bytes 884740
  7.2 4.8 %copy-start.18 = (bf16[768,192]{0,1:T(8,128)(2,1)S(1)}, bf16[768,192]{0,1:T(8,128)(2,1)}, u32[]{:S(2)}) copy-start(bf16[768,192]{0,1:T(8,128)(2,1)} %param.18) | copy-start | bytes 884740
  7.2 5.1 %copy-start.45 = (s32[1,4]{1,0:T(1,128)S(1)}, s32[1,4]{1,0:T(1,128)}, u32[]{:S(2)}) copy-start(s32[1,4]{1,0:T(1,128)} %param.16) | copy-start | bytes 52
  7.3 43.1 %all-reduce.7.cloned.1.call-start = ((), (), s32[]{:S(2)}) async-start(), calls=%async_computation.6 | async-start | bytes 786432 | tf_op jit(solution)/shard_map/psum | solution.py:120
  7.4 5.3 %copy-start.27 = (s32[128,128]{1,0:T(8,128)}, s32[128,128]{1,0:T(8,128)S(1)}, u32[]{:S(2)}) copy-start(s32[128,128]{1,0:T(8,128)S(1)} %compare_select_fusion) | copy-start | bytes 196612
  8.7 4.0 %copy-start.35 = (f32[128]{0:T(128)}, f32[128]{0:T(128)S(1)}, u32[]{:S(2)}) copy-start(f32[128]{0:T(128)S(1)} %add_rsqrt_fusion.1) | copy-start | bytes 1540
  10.1 3.8 %copy-start.6 = (bf16[192,768]{1,0:T(8,128)(2,1)S(1)}, bf16[192,768]{1,0:T(8,128)(2,1)}, u32[]{:S(2)}) copy-start(bf16[192,768]{1,0:T(8,128)(2,1)} %param.20) | copy-start | bytes 884740
  11.7 3.2 copy-start.31
  12.4 39.1 %copy-start.22 = (bf16[128,192]{0,1:T(8,128)(2,1)}, bf16[128,192]{0,1:T(8,128)(2,1)S(1)}, u32[]{:S(2)}) copy-start(bf16[128,192]{0,1:T(8,128)(2,1)S(1)} %convolution_convert_fusion.4) | copy-start | bytes 147460
  13.0 39.0 %copy-start.30 = (f32[768]{0:T(1024)S(1)}, f32[768]{0:T(1024)}, u32[]{:S(2)}) copy-start(f32[768]{0:T(1024)} %param.22) | copy-start | bytes 9220
  55.5 5.6 %copy-start.4 = (bf16[128,768]{1,0:T(8,128)(2,1)S(1)}, bf16[128,768]{1,0:T(8,128)(2,1)}, u32[]{:S(2)}) copy-start(bf16[128,768]{1,0:T(8,128)(2,1)} %param.27) | copy-start | bytes 589828
  55.5 24.9 %all-to-all-start = ((bf16[8,64,768]{2,1,0:T(8,128)(2,1)}), bf16[8,64,768]{2,1,0:T(8,128)(2,1)}, u32[]{:S(2)}, u32[]{:S(2)}) async-start(bf16[8,64,768]{2,1,0:T(8,128)(2,1)} %bitcast.10), calls=%async_computation | async-start | bytes 1572864 | tf_op jit(solution)/shard_map/all_to_all | solution.py:149
  61.9 3.4 %copy-start.37 = (s32[1024]{0:T(1024)S(1)}, s32[1024]{0:T(1024)}, u32[]{:S(2)}) copy-start(s32[1024]{0:T(1024)} %get-tuple-element.37) | copy-start | bytes 12292
  80.4 4.4 %copy-start.44 = (bf16[1,768,768]{2,1,0:T(8,128)(2,1)S(1)}, bf16[1,768,768]{2,1,0:T(8,128)(2,1)}, u32[]{:S(2)}) copy-start(bf16[1,768,768]{2,1,0:T(8,128)(2,1)} %param.25) | copy-start | bytes 3538948
  80.4 23.9 %all-to-all-start.2 = ((bf16[8,64,768]{2,1,0:T(8,128)(2,1)}), bf16[8,64,768]{2,1,0:T(8,128)(2,1)}, u32[]{:S(2)}, u32[]{:S(2)}) async-start(bf16[8,64,768]{2,1,0:T(8,128)(2,1)} %bitcast.22), calls=%async_computation.2 | async-start | bytes 1572864 | tf_op jit(solution)/shard_map/all_to_all | solution.py:184
  84.8 33.4 %reduce-scatter.7.cloned.1.call-start = ((), (), s32[]{:S(2)}) async-start(), calls=%async_computation.7 | async-start | bytes 983040
  93.6 67.9 %reduce-scatter.9.cloned.1.call-start = ((), (), s32[]{:S(2)}) async-start(), calls=%async_computation.8 | async-start | bytes 1966080
  120.4 14.1 %all-to-all-start.1 = ((bf16[8,64,192]{2,1,0:T(8,128)(2,1)}), bf16[8,64,192]{2,1,0:T(8,128)(2,1)S(1)}, u32[]{:S(2)}, u32[]{:S(2)}) async-start(bf16[8,64,192]{2,1,0:T(8,128)(2,1)} %copy.93), calls=%async_computation.1 | async-start | bytes 524288 | tf_op jit(solution)/shard_map/all_to_all | solution.py:159
  159.0 8.2 %copy-start.34 = (f32[128]{0:T(128)S(1)}, f32[128]{0:T(128)}, u32[]{:S(2)}) copy-start(f32[128]{0:T(128)} %copy-done.33) | copy-start | bytes 1540
  159.0 8.2 %copy-start.39 = (f32[128]{0:T(128)S(1)}, f32[128]{0:T(128)}, u32[]{:S(2)}) copy-start(f32[128]{0:T(128)} %copy-done.38) | copy-start | bytes 1540
  159.0 8.2 %copy-start.32 = (s32[128,2]{0,1:T(2,128)S(1)}, s32[128,2]{0,1:T(2,128)}, u32[]{:S(2)}) copy-start(s32[128,2]{0,1:T(2,128)} %param.15) | copy-start | bytes 3076
  163.7 13.1 %all-to-all-start.3 = ((bf16[8,64,192]{2,1,0:T(8,128)(2,1)}), bf16[8,64,192]{2,1,0:T(8,128)(2,1)S(1)}, u32[]{:S(2)}, u32[]{:S(2)}) async-start(bf16[8,64,192]{2,1,0:T(8,128)(2,1)} %copy.95), calls=%async_computation.3 | async-start | bytes 524288 | tf_op jit(solution)/shard_map/all_to_all | solution.py:203
  167.2 148.5 %all-reduce.9.cloned.1.call-start = ((), (), s32[]{:S(2)}) async-start(), calls=%async_computation.9 | async-start | bytes 4718592 | tf_op jit(solution)/shard_map/psum | solution.py:267
  194.7 3.1 copy-start.29
  194.7 3.1 copy-start.41
  205.8 3.7 %copy-start.3 = (bf16[128,768]{1,0:T(8,128)(2,1)S(1)}, bf16[128,768]{1,0:T(8,128)(2,1)}, u32[]{:S(2)}) copy-start(bf16[128,768]{1,0:T(8,128)(2,1)} %copy-done.2) | copy-start | bytes 589828
  205.8 4.0 %copy-start.17 = (bf16[768,192]{0,1:T(8,128)(2,1)S(1)}, bf16[768,192]{0,1:T(8,128)(2,1)}, u32[]{:S(2)}) copy-start(bf16[768,192]{0,1:T(8,128)(2,1)} %param.17) | copy-start | bytes 884740
  210.7 9.1 %copy-start.28 = (s32[128,128]{1,0:T(8,128)S(1)}, s32[128,128]{1,0:T(8,128)}, u32[]{:S(2)}) copy-start(s32[128,128]{1,0:T(8,128)} %copy-done.27) | copy-start | bytes 196612
  315.7 3.7 %copy-start.8 = (f32[192,768]{1,0:T(8,128)S(1)}, f32[192,768]{1,0:T(8,128)}, u32[]{:S(2)}) copy-start(f32[192,768]{1,0:T(8,128)} %get-tuple-element.44) | copy-start | bytes 1769476
  (24 other events, 33.3 us)
Sparse Core Ops, SparseCore 0:
  15.0 35.3 all-reduce.6
  93.7 24.1 reduce-scatter.6
  120.4 34.7 reduce-scatter.8
  205.9 109.7 all-reduce.8
